TPU v7x, 32 devices: a whole 2x2x4 slice. The times are simulated.
32 devices in a mesh: geo: 4 (over y, x), band: 4 (over z), cls: 2 (over core).
Axes of the slice: x: 2, y: 2, z: 4, core: 2. Of those that a mesh axis runs over, the one named last changes fastest.
Arguments:
- mass: bfloat16 [64, 16, 16, 128], P('cls', 'geo', 'band'), may hold values from -6 to 6
- cell_order: int32 [16, 16, 128], P('geo', 'band'), may hold values from 0 to 127, each once within a row
- source_code: int32 [16, 16, 4], P('geo', 'band'), may hold values from 0 to 8
- transport_tiles: bfloat16 [16, 16, 4, 128, 128], P('geo', 'band'), may hold values from -0.25 to 0.25
- ocean_mask: int32 [16, 16], P('geo', 'band'), may hold values 0 or 1
- fragmentation: bfloat16 [64, 64, 16, 16, 128], P(None, None, 'geo', ('band', 'cls')), may hold values from -0.75 to 0.75
Outputs:
- drifted: bfloat16 [64, 16, 16, 128], P('cls', 'geo', 'band')
Inputs may be any that keep to these rules, and one draw needn't show every extreme that they name: cell_order holds each of 0..127 once in every tile. `source_code`: codes 0..8 name the 3 x 3 neighbourhood of tiles.
All inputs are finite; a program needn't handle non-finite values. No bound on the sum of `ocean_mask` on one device may be relied on, other than what follows from the above.
Results may differ from a plain program's by a relative error of at most 0.018.
Values may be sent and summed in bfloat16 or wider, within the bound.
A program may use at most 64 MiB of HBM per device.

v0:
```python
import jax
import jax.numpy as jnp
from jax import lax
from jax.sharding import PartitionSpec as P

ITERS = 4


def extended(cells, sides, width, closed):
    for axis, dim in sides:
        count = lax.axis_size(axis)
        ends = count if closed else count - 1
        head = lax.slice_in_dim(cells, 0, width, axis=dim)
        tail = lax.slice_in_dim(cells, cells.shape[dim] - width, cells.shape[dim], axis=dim)
        cells = jnp.concatenate(
            [
                lax.ppermute(tail, axis, [(i, (i + 1) % count) for i in range(ends)]),
                cells,
                lax.ppermute(head, axis, [((i + 1) % count, i) for i in range(ends)]),
            ],
            axis=dim,
        )
    return cells


def lon_extend(field):
    return extended(field, (("geo", 1),), 1, True)


def apply_tiles(padded, transport_tiles, source_code, ocean_mask):
    tiles_lon = padded.shape[1] - 2
    tiles_lat = padded.shape[2] - 2
    total = jnp.zeros((padded.shape[0], tiles_lon, tiles_lat, padded.shape[3]), jnp.float32)
    for slot in range(transport_tiles.shape[2]):
        picked = jnp.zeros((padded.shape[0], tiles_lon, tiles_lat, padded.shape[3]), padded.dtype)
        for code in range(9):
            dlon = code // 3 - 1
            dlat = code % 3 - 1
            view = padded[:, 1 + dlon : 1 + dlon + tiles_lon, 1 + dlat : 1 + dlat + tiles_lat, :]
            hit = (source_code[:, :, slot] == code)[None, :, :, None]
            picked = jnp.where(hit, view, picked)
        total = total + jnp.einsum(
            "gbij,kgbj->kgbi",
            transport_tiles[:, :, slot],
            picked,
            preferred_element_type=jnp.float32,
        )
    keep = ocean_mask.astype(jnp.float32)[None, :, :, None]
    return (total * keep).astype(jnp.bfloat16)


def fragment(fragmentation, moved):
    total = jnp.einsum("oigbc,igbc->ogbc", fragmentation, moved, preferred_element_type=jnp.float32)
    return total.astype(jnp.bfloat16)


def reorder_cells(mass, cell_order, ocean_mask):
    columns = lax.broadcasted_iota(jnp.int32, cell_order.shape + (mass.shape[3],), 3)
    picker = (cell_order[..., None] == columns).astype(jnp.bfloat16)
    placed = jnp.einsum("kgbj,gbcj->kgbc", mass, picker, preferred_element_type=jnp.float32)
    return placed.astype(jnp.bfloat16) * ocean_mask.astype(jnp.bfloat16)[None, :, :, None]


def shards(mass, cell_order, source_code, transport_tiles, ocean_mask, fragmentation):
    tiled = reorder_cells(mass, cell_order, ocean_mask)
    for step in range(ITERS):
        widened = lon_extend(tiled)
        padded = extended(widened, (("band", 2),), 1, False)
        moved = apply_tiles(padded, transport_tiles, source_code, ocean_mask)
        gathered = lax.all_to_all(moved, "cls", split_axis=2, concat_axis=0, tiled=True)
        fragmented = fragment(fragmentation, gathered)
        tiled = lax.all_to_all(fragmented, "cls", split_axis=0, concat_axis=2, tiled=True)
    return tiled


def solution(mesh):
    placed = (
        P("cls", "geo", "band", None),
        P("geo", "band", None),
        P("geo", "band", None),
        P("geo", "band", None, None, None),
        P("geo", "band"),
        P(None, None, "geo", ("band", "cls"), None),
    )
    return jax.shard_map(
        shards, mesh=mesh, in_specs=placed, out_specs=P("cls", "geo", "band", None), check_vma=False
    )
```

profile of v0, /device:TPU:0, one launch (start us, length us, event | category | flops | bytes accessed | tf_op | source)
XLA Modules:
  0.0 143.3 jit_solution(18423595451460887063)
XLA Ops:
  0.0 0.9 fusion.476
  0.9 1.1 fusion.13
  2.1 3.0 %collective-permute-start = (bf16[32,1,4,128]{3,0,2,1:T(8,128)(2,1)S(1)}, bf16[32,1,4,128]{3,0,2,1:T(8,128)(2,1)S(1)}, u32[]{:S(2)}, u32[]{:S(2)}) collective-permute-start(bf16[32,1,4,128]{3,0,2,1:T(8,128)(2,1)S(1)} %get-tuple-element.63), channel_id=1, source_target_pairs={{0,8},{8,16},{16,24},{24,0},{1,9},{9,17},{17,25},{25,1},{2,10},{10... | collective-permute-start | bytes 98312 | tf_op jit(solution)/shard_map/ppermute | solution.py:17
  5.1 1.0 collective-permute-start.1
  6.1 1.8 %collective-permute-done = bf16[32,1,4,128]{3,0,2,1:T(8,128)(2,1)S(1)} collective-permute-done((bf16[32,1,4,128]{3,0,2,1:T(8,128)(2,1)S(1)}, bf16[32,1,4,128]{3,0,2,1:T(8,128)(2,1)S(1)}, u32[]{:S(2)}, u32[]{:S(2)}) %collective-permute-start) | collective-permute-done | bytes 32800 | tf_op jit(solution)/shard_map/ppermute | solution.py:17
  7.9 1.1 collective-permute-done.1
  9.0 1.3 collective-permute-start.2
  10.3 4.5 %collective-permute-start.3 = (bf16[32,6,1,128]{3,0,2,1:T(8,128)(2,1)S(1)}, bf16[32,6,1,128]{3,0,2,1:T(8,128)(2,1)S(1)}, u32[]{:S(2)}, u32[]{:S(2)}) collective-permute-start(bf16[32,6,1,128]{3,0,2,1:T(8,128)(2,1)S(1)} %get-tuple-element.56), channel_id=1, source_target_pairs={{0,2},{2,4},{4,6},{1,3},{3,5},{5,7},{8,10},{10,12},{12,14},{9,11},... | collective-permute-start | bytes 147464 | tf_op jit(solution)/shard_map/ppermute | solution.py:17
  14.9 3.5 %compare_reduce_fusion.7 = (pred[4,4]{1,0:T(4,128)(4,1)S(1)}, pred[4,4]{1,0:T(4,128)(4,1)S(1)}, pred[4,4]{1,0:T(4,128)(4,1)S(1)}, pred[4,4]{1,0:T(4,128)(4,1)S(1...) fusion(s32[4,4,4]{2,1,0:T(4,128)} %param.8), kind=kLoop, calls=%fused_computation.517 | loop fusion | flops 576 | bytes 832 | tf_op jit(solution)/shard_map/eq | solution.py:40
  18.5 0.7 fusion.32
  19.1 0.7 convolution_add_fusion.11
  19.8 0.7 convolution_add_fusion.10
  20.5 0.4 fusion.14
  20.9 4.0 %all_to_all.144 = bf16[32,4,4,128]{3,0,1,2:T(8,128)(2,1)S(1)} all-to-all(bf16[32,4,4,128]{3,0,1,2:T(8,128)(2,1)S(1)} %copy.61), channel_id=1, replica_groups=mesh['geo'=4,'band'=4,'cls'=2] {'cls'}, dimensions={2} | all-to-all | bytes 262144 | tf_op jit(solution)/shard_map/all_to_all | solution.py:70
  25.0 0.2 copy.118
  25.2 10.4 %fusion = bf16[4,2,128,64]{2,1,0,3:T(2,128)(2,1)S(1)} fusion(f32[4,2,128,64]{2,1,0,3:T(2,128)S(1)} %copy.118, bf16[64,64,4,2,128]{4,3,2,1,0:T(2,128)(2,1)S(1)} %copy-done.1), kind=kLoop, calls=%fused_computation.4 | loop fusion | flops 12517376 | bytes 8781824 | tf_op jit(solution)/shard_map/oigbc,igbc->ogbc/dot_general | solution.py:53
  35.6 3.8 %all_to_all.145 = bf16[64,4,2,128]{3,2,1,0:T(2,128)(2,1)S(1)} all-to-all(bf16[64,4,2,128]{3,2,1,0:T(2,128)(2,1)S(1)} %bitcast.139), channel_id=1, replica_groups=mesh['geo'=4,'band'=4,'cls'=2] {'cls'}, dimensions={0} | all-to-all | bytes 262144 | tf_op jit(solution)/shard_map/all_to_all | solution.py:72
  39.5 2.4 %collective-permute-start.4 = (bf16[32,1,4,128]{3,0,2,1:T(8,128)(2,1)S(1)}, bf16[32,1,4,128]{3,0,2,1:T(8,128)(2,1)S(1)}, u32[]{:S(2)}, u32[]{:S(2)}) collective-permute-start(bf16[32,1,4,128]{3,0,2,1:T(8,128)(2,1)S(1)} %get-tuple-element.61), channel_id=1, source_target_pairs={{0,8},{8,16},{16,24},{24,0},{1,9},{9,17},{17,25},{25,1},{2,10},{10... | collective-permute-start | bytes 98312 | tf_op jit(solution)/shard_map/ppermute | solution.py:17
  42.0 0.5 collective-permute-start.5
  42.5 2.2 %collective-permute-done.4 = bf16[32,1,4,128]{3,0,2,1:T(8,128)(2,1)S(1)} collective-permute-done((bf16[32,1,4,128]{3,0,2,1:T(8,128)(2,1)S(1)}, bf16[32,1,4,128]{3,0,2,1:T(8,128)(2,1)S(1)}, u32[]{:S(2)}, u32[]{:S(2)}) %collective-permute-start.4) | collective-permute-done | bytes 32800 | tf_op jit(solution)/shard_map/ppermute | solution.py:17
  44.7 1.2 collective-permute-done.5
  45.9 1.3 collective-permute-start.6
  47.2 4.5 %collective-permute-start.7 = (bf16[32,6,1,128]{3,0,2,1:T(8,128)(2,1)S(1)}, bf16[32,6,1,128]{3,0,2,1:T(8,128)(2,1)S(1)}, u32[]{:S(2)}, u32[]{:S(2)}) collective-permute-start(bf16[32,6,1,128]{3,0,2,1:T(8,128)(2,1)S(1)} %get-tuple-element.52), channel_id=1, source_target_pairs={{0,2},{2,4},{4,6},{1,3},{3,5},{5,7},{8,10},{10,12},{12,14},{9,11},... | collective-permute-start | bytes 147464 | tf_op jit(solution)/shard_map/ppermute | solution.py:17
  51.7 0.1 collective-permute-done.6
  51.9 1.6 %collective-permute-done.7 = bf16[32,6,1,128]{3,0,2,1:T(8,128)(2,1)S(1)} collective-permute-done((bf16[32,6,1,128]{3,0,2,1:T(8,128)(2,1)S(1)}, bf16[32,6,1,128]{3,0,2,1:T(8,128)(2,1)S(1)}, u32[]{:S(2)}, u32[]{:S(2)}) %collective-permute-start.7) | collective-permute-done | bytes 49184 | tf_op jit(solution)/shard_map/ppermute | solution.py:17
  53.5 0.7 fusion.30
  54.2 0.7 convolution_add_fusion.8
  54.8 0.7 convolution_add_fusion.7
  55.5 0.4 fusion.15
  56.0 3.8 %all_to_all.146 = bf16[32,4,4,128]{3,0,1,2:T(8,128)(2,1)S(1)} all-to-all(bf16[32,4,4,128]{3,0,1,2:T(8,128)(2,1)S(1)} %copy.66), channel_id=1, replica_groups=mesh['geo'=4,'band'=4,'cls'=2] {'cls'}, dimensions={2} | all-to-all | bytes 262144 | tf_op jit(solution)/shard_map/all_to_all | solution.py:70
  59.9 0.2 copy.119
  60.1 10.4 %fusion.1 = bf16[4,2,128,64]{2,1,0,3:T(2,128)(2,1)S(1)} fusion(f32[4,2,128,64]{2,1,0,3:T(2,128)S(1)} %copy.119, bf16[64,64,4,2,128]{4,3,2,1,0:T(2,128)(2,1)S(1)} %copy-done.1), kind=kLoop, calls=%fused_computation.5 | loop fusion | flops 12517376 | bytes 8781824 | tf_op jit(solution)/shard_map/oigbc,igbc->ogbc/dot_general | solution.py:53
  70.5 3.8 %all_to_all.147 = bf16[64,4,2,128]{3,2,1,0:T(2,128)(2,1)S(1)} all-to-all(bf16[64,4,2,128]{3,2,1,0:T(2,128)(2,1)S(1)} %bitcast.140), channel_id=1, replica_groups=mesh['geo'=4,'band'=4,'cls'=2] {'cls'}, dimensions={0} | all-to-all | bytes 262144 | tf_op jit(solution)/shard_map/all_to_all | solution.py:72
  74.4 1.5 %collective-permute-start.8 = (bf16[32,1,4,128]{3,0,2,1:T(8,128)(2,1)S(1)}, bf16[32,1,4,128]{3,0,2,1:T(8,128)(2,1)S(1)}, u32[]{:S(2)}, u32[]{:S(2)}) collective-permute-start(bf16[32,1,4,128]{3,0,2,1:T(8,128)(2,1)S(1)} %get-tuple-element.59), channel_id=1, source_target_pairs={{0,8},{8,16},{16,24},{24,0},{1,9},{9,17},{17,25},{25,1},{2,10},{10... | collective-permute-start | bytes 98312 | tf_op jit(solution)/shard_map/ppermute | solution.py:17
  76.0 1.4 %collective-permute-start.9 = (bf16[32,1,4,128]{3,0,2,1:T(8,128)(2,1)S(1)}, bf16[32,1,4,128]{3,0,2,1:T(8,128)(2,1)S(1)}, u32[]{:S(2)}, u32[]{:S(2)}) collective-permute-start(bf16[32,1,4,128]{3,0,2,1:T(8,128)(2,1)S(1)} %get-tuple-element.60), channel_id=1, source_target_pairs={{8,0},{16,8},{24,16},{0,24},{9,1},{17,9},{25,17},{1,25},{10,2},{18... | collective-permute-start | bytes 98312 | tf_op jit(solution)/shard_map/ppermute | solution.py:19
  77.4 1.9 %collective-permute-done.8 = bf16[32,1,4,128]{3,0,2,1:T(8,128)(2,1)S(1)} collective-permute-done((bf16[32,1,4,128]{3,0,2,1:T(8,128)(2,1)S(1)}, bf16[32,1,4,128]{3,0,2,1:T(8,128)(2,1)S(1)}, u32[]{:S(2)}, u32[]{:S(2)}) %collective-permute-start.8) | collective-permute-done | bytes 32800 | tf_op jit(solution)/shard_map/ppermute | solution.py:17
  79.3 0.6 collective-permute-done.9
  79.9 1.3 collective-permute-start.10
  81.2 4.9 %collective-permute-start.11 = (bf16[32,6,1,128]{3,0,2,1:T(8,128)(2,1)S(1)}, bf16[32,6,1,128]{3,0,2,1:T(8,128)(2,1)S(1)}, u32[]{:S(2)}, u32[]{:S(2)}) collective-permute-start(bf16[32,6,1,128]{3,0,2,1:T(8,128)(2,1)S(1)} %get-tuple-element.48), channel_id=1, source_target_pairs={{0,2},{2,4},{4,6},{1,3},{3,5},{5,7},{8,10},{10,12},{12,14},{9,11},... | collective-permute-start | bytes 147464 | tf_op jit(solution)/shard_map/ppermute | solution.py:17
  86.2 1.6 %collective-permute-done.11 = bf16[32,6,1,128]{3,0,2,1:T(8,128)(2,1)S(1)} collective-permute-done((bf16[32,6,1,128]{3,0,2,1:T(8,128)(2,1)S(1)}, bf16[32,6,1,128]{3,0,2,1:T(8,128)(2,1)S(1)}, u32[]{:S(2)}, u32[]{:S(2)}) %collective-permute-start.11) | collective-permute-done | bytes 49184 | tf_op jit(solution)/shard_map/ppermute | solution.py:17
  87.9 0.7 fusion.28
  88.5 0.7 convolution_add_fusion.5
  89.2 0.7 convolution_add_fusion.4
  89.9 0.4 fusion.16
  90.3 3.8 %all_to_all.148 = bf16[32,4,4,128]{3,0,1,2:T(8,128)(2,1)S(1)} all-to-all(bf16[32,4,4,128]{3,0,1,2:T(8,128)(2,1)S(1)} %copy.71), channel_id=1, replica_groups=mesh['geo'=4,'band'=4,'cls'=2] {'cls'}, dimensions={2} | all-to-all | bytes 262144 | tf_op jit(solution)/shard_map/all_to_all | solution.py:70
  94.2 0.2 copy.120
  94.4 10.4 %fusion.2 = bf16[4,2,128,64]{2,1,0,3:T(2,128)(2,1)S(1)} fusion(f32[4,2,128,64]{2,1,0,3:T(2,128)S(1)} %copy.120, bf16[64,64,4,2,128]{4,3,2,1,0:T(2,128)(2,1)S(1)} %copy-done.1), kind=kLoop, calls=%fused_computation.6 | loop fusion | flops 12517376 | bytes 8781824 | tf_op jit(solution)/shard_map/oigbc,igbc->ogbc/dot_general | solution.py:53
  104.9 3.8 %all_to_all.149 = bf16[64,4,2,128]{3,2,1,0:T(2,128)(2,1)S(1)} all-to-all(bf16[64,4,2,128]{3,2,1,0:T(2,128)(2,1)S(1)} %bitcast.141), channel_id=1, replica_groups=mesh['geo'=4,'band'=4,'cls'=2] {'cls'}, dimensions={0} | all-to-all | bytes 262144 | tf_op jit(solution)/shard_map/all_to_all | solution.py:72
  108.8 1.0 collective-permute-start.12
  109.8 2.0 %collective-permute-start.13 = (bf16[32,1,4,128]{3,0,2,1:T(8,128)(2,1)S(1)}, bf16[32,1,4,128]{3,0,2,1:T(8,128)(2,1)S(1)}, u32[]{:S(2)}, u32[]{:S(2)}) collective-permute-start(bf16[32,1,4,128]{3,0,2,1:T(8,128)(2,1)S(1)} %get-tuple-element.58), channel_id=1, source_target_pairs={{8,0},{16,8},{24,16},{0,24},{9,1},{17,9},{25,17},{1,25},{10,2},{18... | collective-permute-start | bytes 98312 | tf_op jit(solution)/shard_map/ppermute | solution.py:19
  111.8 1.9 %collective-permute-done.12 = bf16[32,1,4,128]{3,0,2,1:T(8,128)(2,1)S(1)} collective-permute-done((bf16[32,1,4,128]{3,0,2,1:T(8,128)(2,1)S(1)}, bf16[32,1,4,128]{3,0,2,1:T(8,128)(2,1)S(1)}, u32[]{:S(2)}, u32[]{:S(2)}) %collective-permute-start.12) | collective-permute-done | bytes 32800 | tf_op jit(solution)/shard_map/ppermute | solution.py:17
  113.7 1.3 collective-permute-start.14
  115.0 4.9 %collective-permute-start.15 = (bf16[32,6,1,128]{3,0,2,1:T(8,128)(2,1)S(1)}, bf16[32,6,1,128]{3,0,2,1:T(8,128)(2,1)S(1)}, u32[]{:S(2)}, u32[]{:S(2)}) collective-permute-start(bf16[32,6,1,128]{3,0,2,1:T(8,128)(2,1)S(1)} %get-tuple-element.44), channel_id=1, source_target_pairs={{0,2},{2,4},{4,6},{1,3},{3,5},{5,7},{8,10},{10,12},{12,14},{9,11},... | collective-permute-start | bytes 147464 | tf_op jit(solution)/shard_map/ppermute | solution.py:17
  119.9 0.1 collective-permute-done.14
  120.0 1.6 %collective-permute-done.15 = bf16[32,6,1,128]{3,0,2,1:T(8,128)(2,1)S(1)} collective-permute-done((bf16[32,6,1,128]{3,0,2,1:T(8,128)(2,1)S(1)}, bf16[32,6,1,128]{3,0,2,1:T(8,128)(2,1)S(1)}, u32[]{:S(2)}, u32[]{:S(2)}) %collective-permute-start.15) | collective-permute-done | bytes 49184 | tf_op jit(solution)/shard_map/ppermute | solution.py:17
  121.7 0.7 fusion.26
  122.4 0.7 convolution_add_fusion.2
  123.0 0.7 convolution_add_fusion.1
  123.7 0.4 fusion.17
  124.2 3.8 %all_to_all.150 = bf16[32,4,4,128]{3,0,1,2:T(8,128)(2,1)S(1)} all-to-all(bf16[32,4,4,128]{3,0,1,2:T(8,128)(2,1)S(1)} %copy.76), channel_id=1, replica_groups=mesh['geo'=4,'band'=4,'cls'=2] {'cls'}, dimensions={2} | all-to-all | bytes 262144 | tf_op jit(solution)/shard_map/all_to_all | solution.py:70
  128.1 0.2 copy.121
  128.3 10.4 %fusion.3 = bf16[4,2,128,64]{2,1,0,3:T(2,128)(2,1)S(1)} fusion(f32[4,2,128,64]{2,1,0,3:T(2,128)S(1)} %copy.121, bf16[64,64,4,2,128]{4,3,2,1,0:T(2,128)(2,1)S(1)} %copy-done.1), kind=kLoop, calls=%fused_computation.7 | loop fusion | flops 12517376 | bytes 8781824 | tf_op jit(solution)/shard_map/oigbc,igbc->ogbc/dot_general | solution.py:53
  138.7 3.8 %all_to_all.151 = bf16[64,4,2,128]{3,2,1,0:T(2,128)(2,1)S(1)} all-to-all(bf16[64,4,2,128]{3,2,1,0:T(2,128)(2,1)S(1)} %bitcast.142), channel_id=1, replica_groups=mesh['geo'=4,'band'=4,'cls'=2] {'cls'}, dimensions={0} | all-to-all | bytes 262144 | tf_op jit(solution)/shard_map/all_to_all | solution.py:72
  142.6 0.7 copy.81
  (42 shorter events, 0.9 us)
Async XLA Ops:
  0.0 0.9 copy-start
  0.0 18.4 %copy-start.2 = (bf16[4,4,4,128,128]{4,3,2,1,0:T(8,128)(2,1)S(1)}, bf16[4,4,4,128,128]{4,3,2,1,0:T(8,128)(2,1)}, u32[]{:S(2)}) copy-start(bf16[4,4,4,128,128]{4,3,2,1,0:T(8,128)(2,1)} %param.9) | copy-start | bytes 6291460
  2.1 5.8 %collective-permute-start = (bf16[32,1,4,128]{3,0,2,1:T(8,128)(2,1)S(1)}, bf16[32,1,4,128]{3,0,2,1:T(8,128)(2,1)S(1)}, u32[]{:S(2)}, u32[]{:S(2)}) collective-permute-start(bf16[32,1,4,128]{3,0,2,1:T(8,128)(2,1)S(1)} %get-tuple-element.63), channel_id=1, source_target_pairs={{0,8},{8,16},{16,24},{24,0},{1,9},{9,17},{17,25},{25,1},{2,10},{10... | collective-permute-start | bytes 98312 | tf_op jit(solution)/shard_map/ppermute | solution.py:17
  5.1 3.9 %collective-permute-start.1 = (bf16[32,1,4,128]{3,0,2,1:T(8,128)(2,1)S(1)}, bf16[32,1,4,128]{3,0,2,1:T(8,128)(2,1)S(1)}, u32[]{:S(2)}, u32[]{:S(2)}) collective-permute-start(bf16[32,1,4,128]{3,0,2,1:T(8,128)(2,1)S(1)} %get-tuple-element.64), channel_id=1, source_target_pairs={{8,0},{16,8},{24,16},{0,24},{9,1},{17,9},{25,17},{1,25},{10,2},{18... | collective-permute-start | bytes 98312 | tf_op jit(solution)/shard_map/ppermute | solution.py:19
  9.0 9.4 %collective-permute-start.2 = (bf16[32,6,1,128]{3,0,2,1:T(8,128)(2,1)S(1)}, bf16[32,6,1,128]{3,0,2,1:T(8,128)(2,1)S(1)}, u32[]{:S(2)}, u32[]{:S(2)}) collective-permute-start(bf16[32,6,1,128]{3,0,2,1:T(8,128)(2,1)S(1)} %get-tuple-element.55), channel_id=1, source_target_pairs={{2,0},{4,2},{6,4},{3,1},{5,3},{7,5},{10,8},{12,10},{14,12},{11,9},... | collective-permute-start | bytes 147464 | tf_op jit(solution)/shard_map/ppermute | solution.py:19
  10.3 8.1 %collective-permute-start.3 = (bf16[32,6,1,128]{3,0,2,1:T(8,128)(2,1)S(1)}, bf16[32,6,1,128]{3,0,2,1:T(8,128)(2,1)S(1)}, u32[]{:S(2)}, u32[]{:S(2)}) collective-permute-start(bf16[32,6,1,128]{3,0,2,1:T(8,128)(2,1)S(1)} %get-tuple-element.56), channel_id=1, source_target_pairs={{0,2},{2,4},{4,6},{1,3},{3,5},{5,7},{8,10},{10,12},{12,14},{9,11},... | collective-permute-start | bytes 147464 | tf_op jit(solution)/shard_map/ppermute | solution.py:17
  19.1 6.1 %copy-start.1 = (bf16[64,64,4,2,128]{4,3,2,1,0:T(2,128)(2,1)S(1)}, bf16[64,64,4,2,128]{4,3,2,1,0:T(2,128)(2,1)}, u32[]{:S(2)}) copy-start(bf16[64,64,4,2,128]{4,3,2,1,0:T(2,128)(2,1)} %param.11) | copy-start | bytes 25165828
  39.5 5.1 %collective-permute-start.4 = (bf16[32,1,4,128]{3,0,2,1:T(8,128)(2,1)S(1)}, bf16[32,1,4,128]{3,0,2,1:T(8,128)(2,1)S(1)}, u32[]{:S(2)}, u32[]{:S(2)}) collective-permute-start(bf16[32,1,4,128]{3,0,2,1:T(8,128)(2,1)S(1)} %get-tuple-element.61), channel_id=1, source_target_pairs={{0,8},{8,16},{16,24},{24,0},{1,9},{9,17},{17,25},{25,1},{2,10},{10... | collective-permute-start | bytes 98312 | tf_op jit(solution)/shard_map/ppermute | solution.py:17
  42.0 3.9 %collective-permute-start.5 = (bf16[32,1,4,128]{3,0,2,1:T(8,128)(2,1)S(1)}, bf16[32,1,4,128]{3,0,2,1:T(8,128)(2,1)S(1)}, u32[]{:S(2)}, u32[]{:S(2)}) collective-permute-start(bf16[32,1,4,128]{3,0,2,1:T(8,128)(2,1)S(1)} %get-tuple-element.62), channel_id=1, source_target_pairs={{8,0},{16,8},{24,16},{0,24},{9,1},{17,9},{25,17},{1,25},{10,2},{18... | collective-permute-start | bytes 98312 | tf_op jit(solution)/shard_map/ppermute | solution.py:19
  45.9 6.0 %collective-permute-start.6 = (bf16[32,6,1,128]{3,0,2,1:T(8,128)(2,1)S(1)}, bf16[32,6,1,128]{3,0,2,1:T(8,128)(2,1)S(1)}, u32[]{:S(2)}, u32[]{:S(2)}) collective-permute-start(bf16[32,6,1,128]{3,0,2,1:T(8,128)(2,1)S(1)} %get-tuple-element.51), channel_id=1, source_target_pairs={{2,0},{4,2},{6,4},{3,1},{5,3},{7,5},{10,8},{12,10},{14,12},{11,9},... | collective-permute-start | bytes 147464 | tf_op jit(solution)/shard_map/ppermute | solution.py:19
  47.2 6.3 %collective-permute-start.7 = (bf16[32,6,1,128]{3,0,2,1:T(8,128)(2,1)S(1)}, bf16[32,6,1,128]{3,0,2,1:T(8,128)(2,1)S(1)}, u32[]{:S(2)}, u32[]{:S(2)}) collective-permute-start(bf16[32,6,1,128]{3,0,2,1:T(8,128)(2,1)S(1)} %get-tuple-element.52), channel_id=1, source_target_pairs={{0,2},{2,4},{4,6},{1,3},{3,5},{5,7},{8,10},{10,12},{12,14},{9,11},... | collective-permute-start | bytes 147464 | tf_op jit(solution)/shard_map/ppermute | solution.py:17
  74.4 4.9 %collective-permute-start.8 = (bf16[32,1,4,128]{3,0,2,1:T(8,128)(2,1)S(1)}, bf16[32,1,4,128]{3,0,2,1:T(8,128)(2,1)S(1)}, u32[]{:S(2)}, u32[]{:S(2)}) collective-permute-start(bf16[32,1,4,128]{3,0,2,1:T(8,128)(2,1)S(1)} %get-tuple-element.59), channel_id=1, source_target_pairs={{0,8},{8,16},{16,24},{24,0},{1,9},{9,17},{17,25},{25,1},{2,10},{10... | collective-permute-start | bytes 98312 | tf_op jit(solution)/shard_map/ppermute | solution.py:17
  76.0 3.9 %collective-permute-start.9 = (bf16[32,1,4,128]{3,0,2,1:T(8,128)(2,1)S(1)}, bf16[32,1,4,128]{3,0,2,1:T(8,128)(2,1)S(1)}, u32[]{:S(2)}, u32[]{:S(2)}) collective-permute-start(bf16[32,1,4,128]{3,0,2,1:T(8,128)(2,1)S(1)} %get-tuple-element.60), channel_id=1, source_target_pairs={{8,0},{16,8},{24,16},{0,24},{9,1},{17,9},{25,17},{1,25},{10,2},{18... | collective-permute-start | bytes 98312 | tf_op jit(solution)/shard_map/ppermute | solution.py:19
  79.9 6.3 %collective-permute-start.10 = (bf16[32,6,1,128]{3,0,2,1:T(8,128)(2,1)S(1)}, bf16[32,6,1,128]{3,0,2,1:T(8,128)(2,1)S(1)}, u32[]{:S(2)}, u32[]{:S(2)}) collective-permute-start(bf16[32,6,1,128]{3,0,2,1:T(8,128)(2,1)S(1)} %get-tuple-element.47), channel_id=1, source_target_pairs={{2,0},{4,2},{6,4},{3,1},{5,3},{7,5},{10,8},{12,10},{14,12},{11,9},... | collective-permute-start | bytes 147464 | tf_op jit(solution)/shard_map/ppermute | solution.py:19
  81.2 6.6 %collective-permute-start.11 = (bf16[32,6,1,128]{3,0,2,1:T(8,128)(2,1)S(1)}, bf16[32,6,1,128]{3,0,2,1:T(8,128)(2,1)S(1)}, u32[]{:S(2)}, u32[]{:S(2)}) collective-permute-start(bf16[32,6,1,128]{3,0,2,1:T(8,128)(2,1)S(1)} %get-tuple-element.48), channel_id=1, source_target_pairs={{0,2},{2,4},{4,6},{1,3},{3,5},{5,7},{8,10},{10,12},{12,14},{9,11},... | collective-permute-start | bytes 147464 | tf_op jit(solution)/shard_map/ppermute | solution.py:17
  108.8 4.9 %collective-permute-start.12 = (bf16[32,1,4,128]{3,0,2,1:T(8,128)(2,1)S(1)}, bf16[32,1,4,128]{3,0,2,1:T(8,128)(2,1)S(1)}, u32[]{:S(2)}, u32[]{:S(2)}) collective-permute-start(bf16[32,1,4,128]{3,0,2,1:T(8,128)(2,1)S(1)} %get-tuple-element.57), channel_id=1, source_target_pairs={{0,8},{8,16},{16,24},{24,0},{1,9},{9,17},{17,25},{25,1},{2,10},{10... | collective-permute-start | bytes 98312 | tf_op jit(solution)/shard_map/ppermute | solution.py:17
  109.8 3.9 %collective-permute-start.13 = (bf16[32,1,4,128]{3,0,2,1:T(8,128)(2,1)S(1)}, bf16[32,1,4,128]{3,0,2,1:T(8,128)(2,1)S(1)}, u32[]{:S(2)}, u32[]{:S(2)}) collective-permute-start(bf16[32,1,4,128]{3,0,2,1:T(8,128)(2,1)S(1)} %get-tuple-element.58), channel_id=1, source_target_pairs={{8,0},{16,8},{24,16},{0,24},{9,1},{17,9},{25,17},{1,25},{10,2},{18... | collective-permute-start | bytes 98312 | tf_op jit(solution)/shard_map/ppermute | solution.py:19
  113.7 6.3 %collective-permute-start.14 = (bf16[32,6,1,128]{3,0,2,1:T(8,128)(2,1)S(1)}, bf16[32,6,1,128]{3,0,2,1:T(8,128)(2,1)S(1)}, u32[]{:S(2)}, u32[]{:S(2)}) collective-permute-start(bf16[32,6,1,128]{3,0,2,1:T(8,128)(2,1)S(1)} %get-tuple-element.43), channel_id=1, source_target_pairs={{2,0},{4,2},{6,4},{3,1},{5,3},{7,5},{10,8},{12,10},{14,12},{11,9},... | collective-permute-start | bytes 147464 | tf_op jit(solution)/shard_map/ppermute | solution.py:19
  115.0 6.6 %collective-permute-start.15 = (bf16[32,6,1,128]{3,0,2,1:T(8,128)(2,1)S(1)}, bf16[32,6,1,128]{3,0,2,1:T(8,128)(2,1)S(1)}, u32[]{:S(2)}, u32[]{:S(2)}) collective-permute-start(bf16[32,6,1,128]{3,0,2,1:T(8,128)(2,1)S(1)} %get-tuple-element.44), channel_id=1, source_target_pairs={{0,2},{2,4},{4,6},{1,3},{3,5},{5,7},{8,10},{10,12},{12,14},{9,11},... | collective-permute-start | bytes 147464 | tf_op jit(solution)/shard_map/ppermute | solution.py:17
where the time goes:
time: 145 us; the launch traced here: 143 us
  other arithmetic  46.5 us (32%)
  starting transfers between devices  37 us (26%)
  blocking collectives  30.8 us (21%)
  waiting for transfers between devices  15.9 us (11%)
  matrix products  10.8 us (7%)
  local copies, waits for them, and re-layouts  1.88 us (1%)
    dot_general x4, other arithmetic, fragment(): jnp.einsum('oigbc,igbc->ogbc', fragmentation, moved, preferred_element_ty...  41.8 us
    ppermute x8, starting transfers between devices, extended(): lax.ppermute(tail, axis, [(i, (i + 1) % count) for i in range(ends)])  26.8 us
    all_to_all x4, blocking collectives, shards(): lax.all_to_all(moved, 'cls', split_axis=2, concat_axis=0, tiled=True)  15.5 us
    all_to_all x4, blocking collectives, shards(): lax.all_to_all(fragmented, 'cls', split_axis=0, concat_axis=2, tiled=True)  15.4 us
    ppermute x8, waiting for transfers between devices, extended(): lax.ppermute(tail, axis, [(i, (i + 1) % count) for i in range(ends)])  12.6 us
    ppermute x8, starting transfers between devices, extended(): lax.ppermute(head, axis, [((i + 1) % count, i) for i in range(ends)])  10.1 us
    dot_general x16, matrix products, apply_tiles(): jnp.einsum('gbij,kgbj->kgbi', transport_tiles[:, :, slot], picked, prefer...  9.7 us
    eq x1, other arithmetic, apply_tiles(): hit = (source_code[:, :, slot] == code)[None, :, :, None]  3.5 us
  transfers between devices with their start and end apart: 16, of which 14 were waited for; matrix products, arithmetic and copies ran while one was open for 2% of the time, Pallas kernels for 0%

commit v1 on v0

v1 whole, which is shorter than its diff:
```python
import functools

import jax
import jax.numpy as jnp
from jax import lax
from jax.experimental import pallas as pl
from jax.experimental.pallas import tpu as pltpu
from jax.sharding import PartitionSpec as P

ITERS = 4
CHUNKS = 2
DIRECTIONS = [(dx, dy) for dx in (-1, 0, 1) for dy in (-1, 0, 1) if (dx, dy) != (0, 0)]
MESH = pl.DeviceIdType.MESH


def kernel(
    dims, lanes, mass, order, code, tiles, mask, frag, out,
    mass_v, wide, order_v, code_s, mask_s, spot_s, tiles_v, frag_v, moved_f, moved_b, result, fin_send, fin_recv,
    local_sem, pair_send, pair_recv, halo_send, halo_recv, *halo,
):
    per, lon, lat, own_lat, classes, slots, cells = dims
    geo_n, band_n, cls_n = lanes
    own = lon * own_lat
    geo, band, cls = lax.axis_index("geo"), lax.axis_index("band"), lax.axis_index("cls")
    row = band * cls_n + cls
    rows_n = band_n * cls_n
    first_lat = cls * own_lat
    sibling = (geo, band, 1 - cls)

    def place(dx, dy):
        to = row + dy
        return (lax.rem(geo + dx + geo_n, geo_n), to // cls_n, lax.rem(to, cls_n))

    def guarded(dy, body):
        if dy == 0:
            body()
        else:
            pl.when((row + 1 < rows_n) if dy > 0 else (row > 0))(body)

    copies = [
        pltpu.make_async_copy(mass, mass_v.at[cls], local_sem.at[0]),
        pltpu.make_async_copy(order, order_v, local_sem.at[1]),
        pltpu.make_async_copy(code, code_s, local_sem.at[2]),
        pltpu.make_async_copy(mask, mask_s, local_sem.at[3]),
        pltpu.make_async_copy(tiles.at[:, pl.ds(first_lat, own_lat)], tiles_v, local_sem.at[4]),
        pltpu.make_async_copy(frag, frag_v, local_sem.at[5]),
    ]
    for copy in copies:
        copy.start()

    @pl.when(row == 0)
    def _():
        for step in range(ITERS):
            for g in range(lon + 2):
                halo[step][g, 0] = jnp.zeros((classes, cells), jnp.bfloat16)

    @pl.when(row + 1 == rows_n)
    def _():
        for step in range(ITERS):
            for g in range(lon + 2):
                halo[step][g, own_lat + 1] = jnp.zeros((classes, cells), jnp.bfloat16)

    barrier = pltpu.get_barrier_semaphore()
    for dx, dy in DIRECTIONS:
        def greet(dx=dx, dy=dy):
            pl.semaphore_signal(barrier, inc=1, device_id=place(dx, dy), device_id_type=MESH)
        guarded(dy, greet)
    greeted = 2 + 3 * (row > 0).astype(jnp.int32) + 3 * (row + 1 < rows_n).astype(jnp.int32)
    pl.semaphore_wait(barrier, greeted)

    pair = pltpu.make_async_remote_copy(
        src_ref=mass, dst_ref=mass_v.at[cls], send_sem=pair_send.at[0], recv_sem=pair_recv.at[0],
        device_id=sibling, device_id_type=MESH,
    )
    pair.start()
    for copy in copies[:4]:
        copy.wait()
    for g in range(lon):
        for h in range(own_lat):
            for s in range(slots):
                at = (g * own_lat + h) * slots + s
                value = code_s[g, first_lat + h, s]
                third = lax.shift_right_logical(value * 11, 5)
                spot_s[0, at] = g + third
                spot_s[1, at] = h + value - 3 * third
    pair.wait()

    for half in range(cls_n):
        wide[half] = mass_v[half].astype(jnp.float32)
    for g in range(lon):
        for h in range(own_lat):
            line = order_v[g, pl.ds(first_lat + h, 1), :]
            hit = lax.broadcasted_iota(jnp.int32, (cells, cells), 0) == line
            keep = mask_s[g, first_lat + h].astype(jnp.float32)
            picker = jnp.where(hit, keep, 0.0).astype(jnp.bfloat16)
            for half in range(cls_n):
                block = wide[half, pl.ds(g * lat + first_lat + h, per, stride=lon * lat), :]
                placed = jnp.dot(block.astype(jnp.bfloat16), picker, preferred_element_type=jnp.float32)
                halo[0][1 + g, 1 + h, half * per:(half + 1) * per, :] = placed.astype(jnp.bfloat16)

    size = classes // CHUNKS

    def message(step, chunk, way):
        dx, dy = DIRECTIONS[way]
        from_lon = {1: pl.ds(lon, 1), -1: pl.ds(1, 1), 0: pl.ds(1, lon)}[dx]
        to_lon = {1: pl.ds(0, 1), -1: pl.ds(lon + 1, 1), 0: pl.ds(1, lon)}[dx]
        from_lat = {1: pl.ds(own_lat, 1), -1: pl.ds(1, 1), 0: pl.ds(1, own_lat)}[dy]
        to_lat = {1: pl.ds(0, 1), -1: pl.ds(own_lat + 1, 1), 0: pl.ds(1, own_lat)}[dy]
        some = pl.ds(chunk * size, size)
        return pltpu.make_async_remote_copy(
            src_ref=halo[step].at[from_lon, from_lat, some],
            dst_ref=halo[step].at[to_lon, to_lat, some],
            send_sem=halo_send.at[step, chunk, way],
            recv_sem=halo_recv.at[step, chunk, way],
            device_id=place(dx, dy),
            device_id_type=MESH,
        )

    def send(step, chunk):
        for way, (dx, dy) in enumerate(DIRECTIONS):
            guarded(dy, lambda way=way: message(step, chunk, way).start())

    def sent(step, chunk):
        for way, (dx, dy) in enumerate(DIRECTIONS):
            guarded(dy, lambda way=way: message(step, chunk, way).wait_send())

    def arrived(step, chunk):
        for way, (dx, dy) in enumerate(DIRECTIONS):
            guarded(-dy, lambda way=way: message(step, chunk, way).wait_recv())

    def transport(step):
        for chunk in range(CHUNKS):
            arrived(step, chunk)
        for g in range(lon):
            for h in range(own_lat):
                total = None
                for s in range(0, slots, 2):
                    at = (g * own_lat + h) * slots + s
                    left = jnp.concatenate(
                        [halo[step][spot_s[0, at + e], spot_s[1, at + e]] for e in range(2)], axis=1
                    )
                    right = jnp.concatenate([tiles_v[g, h, s + e] for e in range(2)], axis=1)
                    term = lax.dot_general(
                        left, right, (((1,), (1,)), ((), ())), preferred_element_type=jnp.float32
                    )
                    total = term if total is None else total + term
                keep = mask_s[g, first_lat + h].astype(jnp.float32)
                moved_f[pl.ds(g * own_lat + h, classes, stride=own), :] = total * keep
        moved_b[...] = moved_f[...].astype(jnp.bfloat16)

    pack = 16
    blocks = classes * own // pack

    def fragment(start, count):
        together = 4

        def some(at, carry):
            o = start + at * together
            for e in range(together):
                base = pl.multiple_of((o + e) * (classes * own), classes * own)
                total = None
                for q in range(0, blocks, 4):
                    terms = [
                        frag_v[pl.ds(base + (q + j) * pack, pack), :] * moved_b[(q + j) * pack:(q + j + 1) * pack, :]
                        for j in range(4)
                    ]
                    four = ((terms[0] + terms[1]) + (terms[2] + terms[3])).astype(jnp.float32)
                    total = four if total is None else total + four
                result[pl.ds(pl.multiple_of((o + e) * own, own), own), :] = total[:own] + total[own:]
            return carry

        lax.fori_loop(0, count // together, some, 0)

    for chunk in range(CHUNKS):
        send(0, chunk)
    copies[4].wait()
    copies[5].wait()

    def one_step(step):
        transport(step)
        for chunk in range(CHUNKS):
            fragment(chunk * size, size)
            for g in range(lon):
                for h in range(own_lat):
                    values = result[pl.ds(chunk * size * own + g * own_lat + h, size, stride=own), :]
                    halo[step + 1][1 + g, 1 + h, chunk * size:(chunk + 1) * size, :] = values.astype(jnp.bfloat16)
            send(step + 1, chunk)
        for chunk in range(CHUNKS):
            sent(step, chunk)

    for step in range(ITERS - 1):
        one_step(step)

    transport(ITERS - 1)
    fragment((1 - cls) * per, per)
    theirs = pl.ds(pl.multiple_of((1 - cls) * per * own, per * own), per * own)
    fin_send[...] = result[theirs, :].astype(jnp.bfloat16)
    last = pltpu.make_async_remote_copy(
        src_ref=fin_send, dst_ref=fin_recv, send_sem=pair_send.at[1], recv_sem=pair_recv.at[1],
        device_id=sibling, device_id_type=MESH,
    )
    last.start()
    fragment(cls * per, per)
    for chunk in range(CHUNKS):
        sent(ITERS - 1, chunk)
    for h in range(own_lat):
        values = result[pl.ds(cls * per * own + h, per * lon, stride=own_lat), :]
        wide[0, pl.ds(cls * own_lat + h, per * lon, stride=lat), :] = values
    last.wait()
    result[0:per * own, :] = fin_recv[...].astype(jnp.float32)
    for h in range(own_lat):
        values = result[pl.ds(h, per * lon, stride=own_lat), :]
        wide[0, pl.ds((1 - cls) * own_lat + h, per * lon, stride=lat), :] = values
    out[...] = wide[0].astype(out.dtype)


def shards(lanes, mass, cell_order, source_code, transport_tiles, ocean_mask, fragmentation):
    per, lon, lat, cells = mass.shape
    classes = fragmentation.shape[0]
    own_lat = fragmentation.shape[3]
    slots = transport_tiles.shape[2]
    own = lon * own_lat
    dims = (per, lon, lat, own_lat, classes, slots, cells)
    cls_n = lanes[2]
    anywhere = pl.BlockSpec(memory_space=pltpu.HBM)
    result = pl.pallas_call(
        functools.partial(kernel, dims, lanes),
        out_shape=jax.ShapeDtypeStruct((per * lon * lat, cells), jnp.bfloat16),
        in_specs=[anywhere] * 6,
        out_specs=pl.BlockSpec(memory_space=pltpu.VMEM),
        scratch_shapes=[
            pltpu.VMEM((cls_n, per * lon * lat, cells), jnp.bfloat16),
            pltpu.VMEM((cls_n, per * lon * lat, cells), jnp.float32),
            pltpu.VMEM((lon, lat, cells), jnp.int32),
            pltpu.SMEM((lon, lat, slots), jnp.int32),
            pltpu.SMEM((lon, lat), jnp.int32),
            pltpu.SMEM((2, own * slots), jnp.int32),
            pltpu.VMEM((lon, own_lat, slots, cells, cells), jnp.bfloat16),
            pltpu.VMEM((classes * classes * own, cells), jnp.bfloat16),
            pltpu.VMEM((classes * own, cells), jnp.float32),
            pltpu.VMEM((classes * own, cells), jnp.bfloat16),
            pltpu.VMEM((classes * own, cells), jnp.float32),
            pltpu.VMEM((per * own, cells), jnp.bfloat16),
            pltpu.VMEM((per * own, cells), jnp.bfloat16),
            pltpu.SemaphoreType.DMA((6,)),
            pltpu.SemaphoreType.DMA((2,)),
            pltpu.SemaphoreType.DMA((2,)),
            pltpu.SemaphoreType.DMA((ITERS, CHUNKS, len(DIRECTIONS))),
            pltpu.SemaphoreType.DMA((ITERS, CHUNKS, len(DIRECTIONS))),
        ] + [pltpu.VMEM((lon + 2, own_lat + 2, classes, cells), jnp.bfloat16)] * ITERS,
        compiler_params=pltpu.CompilerParams(
            collective_id=0, has_side_effects=True, vmem_limit_bytes=56 * 1024 * 1024
        ),
    )(
        mass.reshape(per * lon * lat, cells),
        cell_order,
        source_code,
        transport_tiles,
        ocean_mask,
        fragmentation.reshape(classes * classes * own, cells),
    )
    return result.reshape(per, lon, lat, cells)


def solution(mesh):
    placed = (
        P("cls", "geo", "band", None),
        P("geo", "band", None),
        P("geo", "band", None),
        P("geo", "band", None, None, None),
        P("geo", "band"),
        P(None, None, "geo", ("band", "cls"), None),
    )
    lanes = (mesh.shape["geo"], mesh.shape["band"], mesh.shape["cls"])
    return jax.shard_map(
        functools.partial(shards, lanes),
        mesh=mesh, in_specs=placed, out_specs=P("cls", "geo", "band", None), check_vma=False,
    )
```

time: 145 us -> 37.6 us (0.26); the launches traced: 143 us -> 37.5 us
  other arithmetic: 46.5 us -> 0 us
  starting transfers between devices: 37 us -> 0 us
  Pallas kernels: 0 us -> 35.9 us
  blocking collectives: 30.8 us -> 0 us
  waiting for transfers between devices: 15.9 us -> 0 us
  matrix products: 10.8 us -> 0 us
    dot_general x4 -> x0, other arithmetic: 41.8 us -> none  [fragment(): jnp.einsum('oigbc,igbc->ogbc', fragmentation, moved, preferred_element_ty...]
    ppermute x16 -> x0, starting transfers between devices: 37 us -> none  [the longest x8 26.8 us: extended(): lax.ppermute(tail, axis, [(i, (i + 1) % count) for i in range(ends)])]
    pallas_call x0 -> x1, Pallas kernels: none -> 35.9 us  [shards(): pl.pallas_call(functools.partial(kernel, dims, lanes), out_shape=jax.Shap...]
    all_to_all x8 -> x0, blocking collectives: 30.8 us -> none  [the longest x4 15.5 us: shards(): lax.all_to_all(moved, 'cls', split_axis=2, concat_axis=0, tiled=True)]
    ppermute x16 -> x0, waiting for transfers between devices: 15.9 us -> none  [the longest x8 12.6 us: extended(): lax.ppermute(tail, axis, [(i, (i + 1) % count) for i in range(ends)])]
    dot_general x17 -> x0, matrix products: 10.8 us -> none  [the longest x16 9.7 us: apply_tiles(): jnp.einsum('gbij,kgbj->kgbi', transport_tiles[:, :, slot], picked, prefer...]
    eq x1 -> x0, other arithmetic: 3.5 us -> none  [apply_tiles(): hit = (source_code[:, :, slot] == code)[None, :, :, None]]
  transfers between devices with their start and end apart: 16 -> 0, of which waited for: 14 -> 0; matrix products, arithmetic and copies ran while one was open for 2% -> 0% of each run, Pallas kernels for 0% -> 0%
where the time goes in v1:
time: 37.6 us; the launch traced here: 37.5 us
  Pallas kernels  35.9 us (95%)
  local copies, waits for them, and re-layouts  1.61 us (4%)
    pallas_call x1, Pallas kernels, shards(): pl.pallas_call(functools.partial(kernel, dims, lanes), out_shape=jax.Shap...  35.9 us
    unnamed x1, local copies, waits for them, and re-layouts  1.61 us

profile of v1, /device:TPU:0, one launch (start us, length us, event | category | flops | bytes accessed | tf_op | source)
XLA Modules:
  0.0 37.5 jit_solution(16619304960102313497)
XLA Ops:
  0.0 35.9 %shard_map.64 = bf16[512,128]{1,0:T(8,128)(2,1)} custom-call(bf16[512,128]{1,0:T(8,128)(2,1)} %bitcast.5, s32[4,4,128]{2,1,0:T(4,128)} %order.1, s32[4,4,4]{2,1,0:T(4,128)} %code.1, bf16[4,4,4,128,128]{4,3,2,1,0:T(8,128)(2,1)} %tiles.1, s32[4,4]{1,0:T(4,128)} %mask.1, bf16[32768,128]{1,0:T(8,128)(2,1)} %bitcast.3), custom_call_target="tpu_custom_call" | custom-call | tf_op jit(solution)/shard_map/pallas_call | solution.py:226
  35.9 1.6 %copy.8 = bf16[32,4,4,128]{3,2,1,0:T(4,128)(2,1)} copy(bf16[32,4,4,128]{3,2,1,0:T(4,128)(2,1)} %bitcast.4) | data formatting | bytes 262144

commit v2 on v1

--- a/solution.py
+++ b/solution.py
@@ -15,12 +15,13 @@
 
 def kernel(
     dims, lanes, mass, order, code, tiles, mask, frag, out,
-    mass_v, wide, order_v, code_s, mask_s, spot_s, tiles_v, frag_v, moved_f, moved_b, result, fin_send, fin_recv,
+    mass_v, wide, order_v, code_s, mask_s, spot_s, tiles_v, frag_v, moved_f, result, fin_send, fin_recv,
     local_sem, pair_send, pair_recv, halo_send, halo_recv, *halo,
 ):
     per, lon, lat, own_lat, classes, slots, cells = dims
     geo_n, band_n, cls_n = lanes
     own = lon * own_lat
+    size = classes // CHUNKS
     geo, band, cls = lax.axis_index("geo"), lax.axis_index("band"), lax.axis_index("cls")
     row = band * cls_n + cls
     rows_n = band_n * cls_n
@@ -50,21 +51,26 @@
 
     @pl.when(row == 0)
     def _():
-        for step in range(ITERS):
+        for buffer in halo:
             for g in range(lon + 2):
-                halo[step][g, 0] = jnp.zeros((classes, cells), jnp.bfloat16)
+                buffer[g, 0] = jnp.zeros((size, cells), jnp.bfloat16)
 
     @pl.when(row + 1 == rows_n)
     def _():
-        for step in range(ITERS):
+        for buffer in halo:
             for g in range(lon + 2):
-                halo[step][g, own_lat + 1] = jnp.zeros((classes, cells), jnp.bfloat16)
+                buffer[g, own_lat + 1] = jnp.zeros((size, cells), jnp.bfloat16)
 
     barrier = pltpu.get_barrier_semaphore()
     for dx, dy in DIRECTIONS:
         def greet(dx=dx, dy=dy):
             pl.semaphore_signal(barrier, inc=1, device_id=place(dx, dy), device_id_type=MESH)
         guarded(dy, greet)
+    copies[4].wait()
+    for g in range(lon):
+        for h in range(own_lat):
+            for s in range(slots):
+                tiles_v[g, h, s] = tiles_v[g, h, s].T
     greeted = 2 + 3 * (row > 0).astype(jnp.int32) + 3 * (row + 1 < rows_n).astype(jnp.int32)
     pl.semaphore_wait(barrier, greeted)
 
@@ -96,9 +102,7 @@
             for half in range(cls_n):
                 block = wide[half, pl.ds(g * lat + first_lat + h, per, stride=lon * lat), :]
                 placed = jnp.dot(block.astype(jnp.bfloat16), picker, preferred_element_type=jnp.float32)
-                halo[0][1 + g, 1 + h, half * per:(half + 1) * per, :] = placed.astype(jnp.bfloat16)
-
-    size = classes // CHUNKS
+                halo[half * per // size][1 + g, 1 + h, half * per % size:half * per % size + per, :] = placed.astype(jnp.bfloat16)
 
     def message(step, chunk, way):
         dx, dy = DIRECTIONS[way]
@@ -106,10 +110,10 @@
         to_lon = {1: pl.ds(0, 1), -1: pl.ds(lon + 1, 1), 0: pl.ds(1, lon)}[dx]
         from_lat = {1: pl.ds(own_lat, 1), -1: pl.ds(1, 1), 0: pl.ds(1, own_lat)}[dy]
         to_lat = {1: pl.ds(0, 1), -1: pl.ds(own_lat + 1, 1), 0: pl.ds(1, own_lat)}[dy]
-        some = pl.ds(chunk * size, size)
+        buffer = halo[step * CHUNKS + chunk]
         return pltpu.make_async_remote_copy(
-            src_ref=halo[step].at[from_lon, from_lat, some],
-            dst_ref=halo[step].at[to_lon, to_lat, some],
+            src_ref=buffer.at[from_lon, from_lat],
+            dst_ref=buffer.at[to_lon, to_lat],
             send_sem=halo_send.at[step, chunk, way],
             recv_sem=halo_recv.at[step, chunk, way],
             device_id=place(dx, dy),
@@ -128,90 +132,90 @@
         for way, (dx, dy) in enumerate(DIRECTIONS):
             guarded(-dy, lambda way=way: message(step, chunk, way).wait_recv())
 
-    def transport(step):
-        for chunk in range(CHUNKS):
-            arrived(step, chunk)
+    def transport(step, chunk):
+        arrived(step, chunk)
+        buffer = halo[step * CHUNKS + chunk]
         for g in range(lon):
             for h in range(own_lat):
                 total = None
                 for s in range(0, slots, 2):
                     at = (g * own_lat + h) * slots + s
                     left = jnp.concatenate(
-                        [halo[step][spot_s[0, at + e], spot_s[1, at + e]] for e in range(2)], axis=1
+                        [buffer[spot_s[0, at + e], spot_s[1, at + e]] for e in range(2)], axis=1
                     )
-                    right = jnp.concatenate([tiles_v[g, h, s + e] for e in range(2)], axis=1)
+                    right = jnp.concatenate([tiles_v[g, h, s + e] for e in range(2)], axis=0)
                     term = lax.dot_general(
-                        left, right, (((1,), (1,)), ((), ())), preferred_element_type=jnp.float32
+                        left, right, (((1,), (0,)), ((), ())), preferred_element_type=jnp.float32
                     )
                     total = term if total is None else total + term
                 keep = mask_s[g, first_lat + h].astype(jnp.float32)
-                moved_f[pl.ds(g * own_lat + h, classes, stride=own), :] = total * keep
-        moved_b[...] = moved_f[...].astype(jnp.bfloat16)
+                moved_f[pl.ds(g * own_lat + h, size, stride=own), :] = total * keep
 
     pack = 16
-    blocks = classes * own // pack
-
-    def fragment(start, count):
-        together = 4
+    blocks = size * own // pack
+
+    def fragment(chunk, start, count):
+        together = 8
+        moved = moved_f[...].astype(jnp.bfloat16)
 
         def some(at, carry):
-            o = start + at * together
             for e in range(together):
-                base = pl.multiple_of((o + e) * (classes * own), classes * own)
+                o = start + at * together + e
+                base = pl.multiple_of((o * classes + chunk * size) * own, size * own)
                 total = None
-                for q in range(0, blocks, 4):
-                    terms = [
-                        frag_v[pl.ds(base + (q + j) * pack, pack), :] * moved_b[(q + j) * pack:(q + j + 1) * pack, :]
-                        for j in range(4)
-                    ]
-                    four = ((terms[0] + terms[1]) + (terms[2] + terms[3])).astype(jnp.float32)
+                block = frag_v[pl.ds(base, size * own), :] * moved
+                half = block[:size * own // 2] + block[size * own // 2:]
+                half = (half[:size * own // 4] + half[size * own // 4:]).astype(jnp.float32)
+                for q in range(0, blocks // 4):
+                    four = half[q * pack:(q + 1) * pack]
                     total = four if total is None else total + four
-                result[pl.ds(pl.multiple_of((o + e) * own, own), own), :] = total[:own] + total[own:]
+                spot = pl.ds(pl.multiple_of(o * own, own), own)
+                total = total[:own] + total[own:]
+                result[spot, :] = total if chunk == 0 else result[spot, :] + total
             return carry
 
         lax.fori_loop(0, count // together, some, 0)
 
     for chunk in range(CHUNKS):
         send(0, chunk)
-    copies[4].wait()
     copies[5].wait()
 
-    def one_step(step):
-        transport(step)
+    def early(step):
+        for chunk in range(CHUNKS - 1):
+            transport(step, chunk)
+            fragment(chunk, 0, classes)
+        transport(step, CHUNKS - 1)
+
+    for step in range(ITERS - 1):
+        early(step)
         for chunk in range(CHUNKS):
-            fragment(chunk * size, size)
+            fragment(CHUNKS - 1, chunk * size, size)
             for g in range(lon):
                 for h in range(own_lat):
                     values = result[pl.ds(chunk * size * own + g * own_lat + h, size, stride=own), :]
-                    halo[step + 1][1 + g, 1 + h, chunk * size:(chunk + 1) * size, :] = values.astype(jnp.bfloat16)
+                    halo[(step + 1) * CHUNKS + chunk][1 + g, 1 + h] = values.astype(jnp.bfloat16)
             send(step + 1, chunk)
         for chunk in range(CHUNKS):
             sent(step, chunk)
 
-    for step in range(ITERS - 1):
-        one_step(step)
-
-    transport(ITERS - 1)
-    fragment((1 - cls) * per, per)
-    theirs = pl.ds(pl.multiple_of((1 - cls) * per * own, per * own), per * own)
-    fin_send[...] = result[theirs, :].astype(jnp.bfloat16)
+    early(ITERS - 1)
+
+    def half_of(which):
+        return result[pl.ds(pl.multiple_of(which * per * own, per * own), per * own), :].astype(jnp.bfloat16)
+
+    fragment(CHUNKS - 1, (1 - cls) * per, per)
+    fin_send[...] = half_of(1 - cls)
     last = pltpu.make_async_remote_copy(
         src_ref=fin_send, dst_ref=fin_recv, send_sem=pair_send.at[1], recv_sem=pair_recv.at[1],
         device_id=sibling, device_id_type=MESH,
     )
     last.start()
-    fragment(cls * per, per)
+    fragment(CHUNKS - 1, cls * per, per)
+    out[cls] = half_of(cls)
     for chunk in range(CHUNKS):
         sent(ITERS - 1, chunk)
-    for h in range(own_lat):
-        values = result[pl.ds(cls * per * own + h, per * lon, stride=own_lat), :]
-        wide[0, pl.ds(cls * own_lat + h, per * lon, stride=lat), :] = values
     last.wait()
-    result[0:per * own, :] = fin_recv[...].astype(jnp.float32)
-    for h in range(own_lat):
-        values = result[pl.ds(h, per * lon, stride=own_lat), :]
-        wide[0, pl.ds((1 - cls) * own_lat + h, per * lon, stride=lat), :] = values
-    out[...] = wide[0].astype(out.dtype)
+    out[1 - cls] = fin_recv[...]
 
 
 def shards(lanes, mass, cell_order, source_code, transport_tiles, ocean_mask, fragmentation):
@@ -225,7 +229,7 @@
     anywhere = pl.BlockSpec(memory_space=pltpu.HBM)
     result = pl.pallas_call(
         functools.partial(kernel, dims, lanes),
-        out_shape=jax.ShapeDtypeStruct((per * lon * lat, cells), jnp.bfloat16),
+        out_shape=jax.ShapeDtypeStruct((cls_n, per * own, cells), jnp.bfloat16),
         in_specs=[anywhere] * 6,
         out_specs=pl.BlockSpec(memory_space=pltpu.VMEM),
         scratch_shapes=[
@@ -237,8 +241,7 @@
             pltpu.SMEM((2, own * slots), jnp.int32),
             pltpu.VMEM((lon, own_lat, slots, cells, cells), jnp.bfloat16),
             pltpu.VMEM((classes * classes * own, cells), jnp.bfloat16),
-            pltpu.VMEM((classes * own, cells), jnp.float32),
-            pltpu.VMEM((classes * own, cells), jnp.bfloat16),
+            pltpu.VMEM((classes // CHUNKS * own, cells), jnp.float32),
             pltpu.VMEM((classes * own, cells), jnp.float32),
             pltpu.VMEM((per * own, cells), jnp.bfloat16),
             pltpu.VMEM((per * own, cells), jnp.bfloat16),
@@ -247,7 +250,7 @@
             pltpu.SemaphoreType.DMA((2,)),
             pltpu.SemaphoreType.DMA((ITERS, CHUNKS, len(DIRECTIONS))),
             pltpu.SemaphoreType.DMA((ITERS, CHUNKS, len(DIRECTIONS))),
-        ] + [pltpu.VMEM((lon + 2, own_lat + 2, classes, cells), jnp.bfloat16)] * ITERS,
+        ] + [pltpu.VMEM((lon + 2, own_lat + 2, classes // CHUNKS, cells), jnp.bfloat16)] * (ITERS * CHUNKS),
         compiler_params=pltpu.CompilerParams(
             collective_id=0, has_side_effects=True, vmem_limit_bytes=56 * 1024 * 1024
         ),
@@ -259,7 +262,8 @@
         ocean_mask,
         fragmentation.reshape(classes * classes * own, cells),
     )
-    return result.reshape(per, lon, lat, cells)
+    result = result.reshape(cls_n, per, lon, own_lat, cells)
+    return jnp.moveaxis(result, 0, 2).reshape(per, lon, lat, cells)
 
 
 def solution(mesh):

time: 37.6 us -> 34.2 us (0.910)
  Pallas kernels: 35.9 us -> 32.4 us
    pallas_call x1, Pallas kernels: 35.9 us -> 32.4 us  [shards(): pl.pallas_call(functools.partial(kernel, dims, lanes), out_shape=jax.Shap...]
    transpose x0 -> x1, local copies, waits for them, and re-layouts: none -> 1.65 us  [shards(): return jnp.moveaxis(result, 0, 2).reshape(per, lon, lat, cells)]
    unnamed x1 -> x0, local copies, waits for them, and re-layouts: 1.61 us -> none
where the time goes in v2:
time: 34.2 us; the launch traced here: 34.1 us
  Pallas kernels  32.4 us (95%)
  local copies, waits for them, and re-layouts  1.65 us (5%)
    pallas_call x1, Pallas kernels, shards(): pl.pallas_call(functools.partial(kernel, dims, lanes), out_shape=jax.Shap...  32.4 us
    transpose x1, local copies, waits for them, and re-layouts, shards(): return jnp.moveaxis(result, 0, 2).reshape(per, lon, lat, cells)  1.65 us

profile of v2, /device:TPU:0, one launch (start us, length us, event | category | flops | bytes accessed | tf_op | source)
XLA Modules:
  0.0 34.1 jit_solution(13699525172020205272)
XLA Ops:
  0.0 32.4 %shard_map.64 = bf16[2,256,128]{2,1,0:T(8,128)(2,1)} custom-call(bf16[512,128]{1,0:T(8,128)(2,1)} %bitcast.8, s32[4,4,128]{2,1,0:T(4,128)} %order.1, s32[4,4,4]{2,1,0:T(4,128)} %code.1, bf16[4,4,4,128,128]{4,3,2,1,0:T(8,128)(2,1)} %tiles.1, s32[4,4]{1,0:T(4,128)} %mask.1, bf16[32768,128]{1,0:T(8,128)(2,1)} %bitcast.6), custom_call_target="tpu_custom_call" | custom-call | tf_op jit(solution)/shard_map/pallas_call | solution.py:230
  32.4 1.7 %copy.7 = bf16[32,4,2,2,128]{4,3,2,1,0:T(2,128)(2,1)} copy(bf16[32,4,2,2,128]{4,3,1,0,2:T(2,128)(2,1)} %bitcast.7) | data formatting | bytes 262144 | tf_op jit(solution)/shard_map/transpose | solution.py:266
